TPU v7x, 32 devices: a whole 2x2x4 slice. The times are simulated.
32 devices in a mesh: tm: 32 (over z, y, x, core), sta: 1.
Axes of the slice: x: 2, y: 2, z: 4, core: 2. Of those that a mesh axis runs over, the one named last changes fastest.
Arguments:
- record: float32 [192, 16384], P('sta', 'tm'), may hold values from -200 to 200
- owner: int32 [96, 1], replicated, may hold values from 0 to 31; in each aligned block of 32 rows (0 to 31, 32 to 63, ...) at most 2 rows name the same one
- offset: int32 [96], replicated, may hold values from 0 to 511
- station: int32 [192], P('sta'), may hold values from 0 to 63, as said below
- valid: int32 [192], P('sta'), may hold values 0 or 1
Outputs:
- stack: float32 [3, 32, 16384], P(None, 'sta', 'tm')
Inputs may be any that keep to these rules, and one draw needn't show every extreme that they name: `owner`: among the 32 templates of one step (rows i * 32 to i * 32 + 31) no time block is named more than 2 times, and some block is named exactly 2 times in some step. Every station number names exactly 3 channels.
All inputs are finite; a program needn't handle non-finite values. No bound on the sum of `valid` on one device may be relied on, other than what follows from the above.
Results may differ from a plain program's by a relative error of at most 0.0015.
Values may be sent and summed in bfloat16 or wider, within the bound.
A program may use at most 64 MiB of HBM per device.

v0:
```python
import math

import jax
import jax.numpy as jnp
from jax import lax
from jax.sharding import PartitionSpec as P

WIN = 100
TPL_STEP = 32
NSTEP = 3


EPSILON = 1e-05


def shifted(array, axis, by):
    length = lax.axis_size(axis)
    pairs = [(i, i + by) for i in range(length) if 0 <= i + by < length]
    return lax.ppermute(array, axis, pairs)


def normalize(pieces):
    values = pieces.astype(jnp.float32)
    centred = values - jnp.mean(values, axis=-1, keepdims=True)
    spread = jnp.sqrt(jnp.mean(centred * centred, axis=-1, keepdims=True) + EPSILON)
    return (centred / (WIN * spread)).astype(jnp.bfloat16)


def body(record, owner, offset, station, valid):
    ch_dev, samp_dev = record.shape
    rounded = record.astype(jnp.bfloat16)
    edge_cells = shifted(rounded[:, : WIN - 1], "tm", -1)
    extended = jnp.concatenate([rounded, edge_cells], axis=1)
    stations = ch_dev * lax.axis_size("sta") // 3
    station_table = (station[:, None] == jnp.arange(stations, dtype=jnp.int32)[None, :]).astype(
        jnp.float32
    )
    present = valid.astype(jnp.float32)
    local_counts = jnp.dot(present, station_table, precision=lax.Precision.HIGHEST)
    counts = lax.psum(local_counts, "sta")
    own_counts = jnp.dot(station_table, counts, precision=lax.Precision.HIGHEST)
    weight = present / jnp.maximum(own_counts, 1.0)
    position = lax.axis_index("tm")
    row_len = ch_dev * WIN

    def template_at(first_sample):
        return normalize(lax.dynamic_slice_in_dim(extended, first_sample, WIN, 1)).reshape(row_len)

    def fetch_step(step_number):
        first_row = step_number * TPL_STEP
        own_step = owner[first_row : first_row + TPL_STEP, 0]
        off_step = offset[first_row : first_row + TPL_STEP]
        capacity = max(2, 2 * TPL_STEP // lax.axis_size("tm"))
        template_index = jnp.arange(TPL_STEP, dtype=jnp.int32)
        earlier = (own_step[None, :] == own_step[:, None]) & (
            template_index[None, :] < template_index[:, None]
        )
        slot_rank = jnp.sum(earlier.astype(jnp.int32), axis=1)
        owned_here = own_step == position
        slot_pick = owned_here[None, :] & (
            slot_rank[None, :] == jnp.arange(capacity, dtype=jnp.int32)[:, None]
        )
        slot_start = jnp.sum(jnp.where(slot_pick, off_step[None, :], 0), axis=1)
        filled = jnp.any(slot_pick, axis=1)
        slot_rows = jax.vmap(template_at)(slot_start)
        slot_rows = jnp.where(filled[:, None], slot_rows, jnp.zeros_like(slot_rows))
        everyone = lax.all_gather(slot_rows, "tm", axis=0, tiled=True)
        return jnp.take(everyone, own_step * capacity + slot_rank, axis=0)

    block_size = 8
    block_count = ch_dev // block_size
    factor = 1.0 / math.sqrt(stations)
    fetched = jnp.concatenate([fetch_step(step_number) for step_number in range(NSTEP)], axis=0)
    row_count = fetched.shape[0]
    shaped = fetched.reshape(row_count, block_count, block_size * WIN)

    def add_block(running, block_index):
        channel_rows = lax.dynamic_slice_in_dim(extended, block_index * block_size, block_size, 0)
        hankel = jnp.stack([channel_rows[:, k : k + samp_dev] for k in range(WIN)], axis=1)
        values = hankel.astype(jnp.float32)
        window_mean = jnp.mean(values, axis=1)
        window_square = jnp.mean(values * values, axis=1)
        inverse = 1.0 / jnp.sqrt(
            jnp.maximum(window_square - window_mean * window_mean, 0.0) + EPSILON
        )
        scaled = lax.dynamic_slice_in_dim(weight, block_index * block_size, block_size, 0)
        window = (values * (scaled[:, None] * inverse)[:, None, :]).astype(jnp.bfloat16)
        template_part = lax.dynamic_index_in_dim(shaped, block_index, 1, keepdims=False)
        product = jnp.dot(
            template_part,
            window.reshape(block_size * WIN, samp_dev),
            preferred_element_type=jnp.float32,
        )
        return (running + product, None)

    running, unused = lax.scan(
        add_block,
        jnp.zeros((row_count, samp_dev), jnp.float32),
        jnp.arange(block_count, dtype=jnp.int32),
    )
    partial_stack = running.reshape(NSTEP, TPL_STEP, samp_dev)
    summed = lax.psum_scatter(partial_stack, "sta", scatter_dimension=1, tiled=True)
    return summed * factor


def solution(mesh):
    placed = (P("sta", "tm"), P(), P(), P("sta"), P("sta"))
    return jax.shard_map(
        body, mesh=mesh, in_specs=placed, out_specs=P(None, "sta", "tm"), check_vma=False
    )
```

profile of v0, /device:TPU:0, one launch (start us, length us, event | category | flops | bytes accessed | tf_op | source)
XLA Modules:
  0.0 561.6 jit_solution(5104861693681272544)
XLA Ops:
  7.6 1.3 collective-permute-start
  16.4 2.9 while.15
  21.1 2.5 while.14
  24.0 2.9 while.16
  30.1 52.1 %all-gather.9.cloned.1.call-done = bf16[32,2,19200]{2,1,0:T(2,128)(2,1)} async-done(((bf16[1,2,19200]{2,1,0:T(2,128)(2,1)}), bf16[32,2,19200]{2,1,0:T(2,128)(2,1)}) %all-gather.9.cloned.1.call-update) | async-done | bytes 2457616 | tf_op jit(solution)/shard_map/all_gather | solution.py:67
  82.2 2.9 reshape.268
  85.1 2.4 gather_fusion.1
  87.5 2.5 broadcast_select_fusion.1
  90.1 51.4 %all-gather.7.cloned.1.call-done = bf16[32,2,19200]{2,1,0:T(2,128)(2,1)} async-done(((bf16[1,2,19200]{2,1,0:T(2,128)(2,1)}), bf16[32,2,19200]{2,1,0:T(2,128)(2,1)}) %all-gather.7.cloned.1.call-update) | async-done | bytes 2457616 | tf_op jit(solution)/shard_map/all_gather | solution.py:67
  141.5 2.9 reshape.266
  144.4 2.4 gather_fusion
  146.8 2.5 broadcast_select_fusion.2
  149.4 51.4 %all-gather.11.cloned.1.call-done = bf16[32,2,19200]{2,1,0:T(2,128)(2,1)} async-done(((bf16[1,2,19200]{2,1,0:T(2,128)(2,1)}), bf16[32,2,19200]{2,1,0:T(2,128)(2,1)}) %all-gather.11.cloned.1.call-update) | async-done | bytes 2457616 | tf_op jit(solution)/shard_map/all_gather | solution.py:67
  200.7 2.9 reshape.270
  203.7 2.4 gather_fusion.2
  206.1 1.6 broadcast_select_fusion
  208.1 1.9 pad_maximum_fusion
  210.0 9.3 %reshape.180 = bf16[96,24,800]{2,1,0:T(8,128)(2,1)} reshape(bf16[96,19200]{1,0:T(8,128)(2,1)} %pad_maximum_fusion) | data formatting | bytes 7372800 | tf_op jit(solution)/shard_map/reshape | solution.py:75
  219.3 4.7 copy.23
  224.0 330.4 %while.17 = (s32[]{:T(128)}, f32[96,512]{1,0:T(8,128)S(1)}, s32[24]{0:T(128)S(1)}, bf16[96,24,800]{2,0,1:T(8,128)(2,1)}, bf16[192,611]{1,0:T(8,128)(2,1)S(1)}, /...) while((s32[]{:T(128)}, f32[96,512]{1,0:T(8,128)S(1)}, ...), condition=%wide.region_18.20_spmd.clone, body=%wide.region_15.19_spmd.clone.sunk | while | flops 81629296 | bytes 8858643 | solution.py:96
  236.5 1.2 convolution_add_fusion.2
  264.0 1.2 convolution_add_fusion.2
  277.8 1.2 convolution_add_fusion.2
  484.3 1.2 convolution_add_fusion.2
  (2676 shorter events, 283.6 us)
Async XLA Ops:
  6.5 75.7 %all-gather.9.cloned.1.call-start = ((), (), s32[]{:S(2)}) async-start(), calls=%async_computation.1 | async-start | bytes 2534400 | tf_op jit(solution)/shard_map/all_gather | solution.py:67
  7.6 8.8 %collective-permute-start = (bf16[192,99]{1,0:T(8,128)(2,1)S(1)}, bf16[192,99]{1,0:T(8,128)(2,1)S(1)}, u32[]{:S(2)}, u32[]{:S(2)}) collective-permute-start(bf16[192,99]{1,0:T(8,128)(2,1)S(1)} %slice.467), channel_id=1, source_target_pairs={{1,0},{2,1},{3,2},{4,3},{5,4},{6,5},{7,6},{8,7},{9,8},{10,9},{11,1... | collective-permute-start | bytes 114056 | tf_op jit(solution)/shard_map/ppermute | solution.py:19
  21.0 120.5 %all-gather.7.cloned.1.call-start = ((), (), s32[]{:S(2)}) async-start(), calls=%async_computation | async-start | bytes 2534400 | tf_op jit(solution)/shard_map/all_gather | solution.py:67
  28.4 172.4 %all-gather.11.cloned.1.call-start = ((), (), s32[]{:S(2)}) async-start(), calls=%async_computation.2 | async-start | bytes 2534400 | tf_op jit(solution)/shard_map/all_gather | solution.py:67
  206.1 1.7 copy-start.1
  206.1 2.0 copy-start.2
  219.3 4.7 copy-start
Sparse Core Ops, SparseCore 0:
  21.1 61.0 all-gather.8
  85.0 56.4 all-gather.6
  144.3 56.4 all-gather.10
where the time goes:
time: 564 us; the launch traced here: 562 us
  local copies, waits for them, and re-layouts  266 us (47%)
  waiting for transfers between devices  155 us (27%)
  loops' own time  65.1 us (12%)
  matrix products  31.4 us (6%)
  other arithmetic  29.1 us (5%)
  between operations  13.3 us (2%)
    while x2376, local copies, waits for them, and re-layouts  197 us
    all_gather x3, waiting for transfers between devices, fetch_step(): everyone = lax.all_gather(slot_rows, 'tm', axis=0, tiled=True)  155 us
    another operation x1, loops' own time, body(): lax.scan(add_block, jnp.zeros((row_count, samp_dev), jnp.float32), jnp.ar...  65 us
    dot_general x24, matrix products, add_block(): jnp.dot(template_part, window.reshape(block_size * WIN, samp_dev), prefer...  29.6 us
    unnamed x16, local copies, waits for them, and re-layouts  14.1 us
    dynamic_slice x24, local copies, waits for them, and re-layouts, body(): lax.scan(add_block, jnp.zeros((row_count, samp_dev), jnp.float32), jnp.ar...  14.1 us
  transfers between devices with their start and end apart: 4, of which 3 were waited for; matrix products, arithmetic and copies ran while one was open for 6% of the time, Pallas kernels for 0%

commit v1 on v0

v1 whole, which is shorter than its diff:
```python
import functools
import math

import jax
import jax.numpy as jnp
from jax import lax
from jax.experimental import pallas as pl
from jax.experimental.pallas import tpu as pltpu
from jax.sharding import PartitionSpec as P

WIN = 100
TPL_STEP = 32
NSTEP = 3
EPSILON = 1e-05
GROUP = 8
SHIFTS = 5
LANES = 128
TAIL = 128
MESH = pl.DeviceIdType.MESH
VMEM = pl.BlockSpec(memory_space=pltpu.VMEM)
SMEM = pl.BlockSpec(memory_space=pltpu.SMEM)


def exchange_kernel(n, mine_ref, all_ref, send_sem, recv_sem, own_sem):
    me = lax.axis_index("tm")
    barrier = pltpu.get_barrier_semaphore()

    def greet(d, carry):
        pl.semaphore_signal(
            barrier, inc=1, device_id={"tm": lax.rem(me + d, n)}, device_id_type=MESH
        )
        return carry

    lax.fori_loop(1, n, greet, 0)
    own = pltpu.make_async_copy(mine_ref.at[lax.rem(me, GROUP)], all_ref.at[me], own_sem)
    own.start()
    pl.semaphore_wait(barrier, n - 1)

    def send(d, carry):
        to = lax.rem(me + d, n)
        pltpu.make_async_remote_copy(
            src_ref=mine_ref.at[lax.rem(to, GROUP)],
            dst_ref=all_ref.at[me],
            send_sem=send_sem.at[d],
            recv_sem=recv_sem.at[me],
            device_id={"tm": to},
            device_id_type=MESH,
        ).start()
        return carry

    lax.fori_loop(1, n, send, 0)

    def finish(d, carry):
        source = lax.rem(me + n - d, n)
        copy = pltpu.make_async_remote_copy(
            src_ref=mine_ref.at[0],
            dst_ref=all_ref.at[source],
            send_sem=send_sem.at[d],
            recv_sem=recv_sem.at[source],
            device_id={"tm": source},
            device_id_type=MESH,
        )
        copy.wait_send()
        copy.wait_recv()
        return carry

    lax.fori_loop(1, n, finish, 0)
    own.wait()


def exchange(mine, n):
    return pl.pallas_call(
        functools.partial(exchange_kernel, n),
        out_shape=jax.ShapeDtypeStruct((n,) + mine.shape[1:], mine.dtype),
        in_specs=[VMEM],
        out_specs=VMEM,
        scratch_shapes=[
            pltpu.SemaphoreType.DMA((n,)),
            pltpu.SemaphoreType.DMA((n,)),
            pltpu.SemaphoreType.DMA,
        ],
        compiler_params=pltpu.CompilerParams(
            collective_id=0, has_side_effects=True, vmem_limit_bytes=32 * 1024 * 1024
        ),
    )(mine)


def ahead(array, by):
    return pltpu.roll(array, array.shape[1] - by, 1) if by else array


def window_sum(x):
    two = x + ahead(x, 1)
    four = two + ahead(two, 2)
    eight = four + ahead(four, 4)
    sixteen = eight + ahead(eight, 8)
    half = sixteen + ahead(sixteen, 16)
    full = half + ahead(half, 32)
    return full + ahead(half, 64) + ahead(four, 96)


def correlate_kernel(
    n, samp, factor, plane_ref, start_ref, all_ref, weight_ref, out_ref,
    chan, rows, raw, tpl, gain, win,
):
    parts = all_ref.shape[1] // 2
    half = samp // 2
    rows_in = SHIFTS * parts
    steps = WIN // SHIFTS
    count = start_ref.shape[0]
    total = n * samp

    def spread(j, carry):
        block = all_ref[j].astype(jnp.float32)
        chan[:, pl.ds(pl.multiple_of(j * samp, samp), half)] = block[:parts]
        chan[:, pl.ds(pl.multiple_of(j * samp + half, half), half)] = block[parts:]
        return carry

    lax.fori_loop(0, n, spread, 0)
    chan[:, pl.ds(total, TAIL)] = jnp.zeros((parts, TAIL), jnp.float32)

    def turn(b, carry):
        at = pl.multiple_of(b * samp, samp)
        values = chan[:, pl.ds(at, samp + TAIL)]
        pieces = [ahead(values, k)[:, :samp] for k in range(SHIFTS)]
        pieces.append(jnp.zeros((LANES - rows_in, samp), jnp.float32))
        rows[pl.ds(at, samp), :] = jnp.concatenate(pieces, axis=0).T
        return carry

    lax.fori_loop(0, n, turn, 0)
    rows[pl.ds(total, TAIL), :] = jnp.zeros((TAIL, LANES), jnp.float32)

    def pick(t, carry):
        raw[pl.ds(t, 24, stride=count), :] = rows[pl.ds(start_ref[t], 24, stride=SHIFTS), :]
        return carry

    lax.fori_loop(0, count, pick, 0)
    lane_a = lax.broadcasted_iota(jnp.int32, (LANES, LANES), 0)
    lane_b = lax.broadcasted_iota(jnp.int32, (LANES, LANES), 1)
    same = (lax.rem(lane_a, parts) == lax.rem(lane_b, parts)) & (
        (lane_a < rows_in) & (lane_b < rows_in)
    )
    fold = jnp.where(same, 1.0, 0.0).astype(jnp.float32)

    def folded(x):
        return jnp.dot(
            x, fold, precision=lax.Precision.HIGHEST, preferred_element_type=jnp.float32
        )

    sums = raw[pl.ds(0, count), :]
    for j in range(1, steps):
        sums = sums + raw[pl.ds(j * count, count), :]
    mean = folded(sums) / WIN
    square = jnp.zeros_like(mean)
    for j in range(steps):
        centred = raw[pl.ds(j * count, count), :] - mean
        square = square + centred * centred
    spread_of = jnp.sqrt(folded(square) / WIN + EPSILON)
    scale = 1.0 / (WIN * spread_of)
    for j in range(steps):
        value = (raw[pl.ds(j * count, count), :] - mean) * scale
        tpl[pl.ds(0, count), pl.ds(j * LANES, LANES)] = value.astype(jnp.bfloat16)
    tpl[pl.ds(count, LANES - count), :] = jnp.zeros(
        (LANES - count, tpl.shape[1]), jnp.bfloat16
    )
    weight = weight_ref[...]
    first = plane_ref[0] * (GROUP * samp)
    sub = 64

    def stack(i, carry):
        base = pl.multiple_of(first + i * samp, samp)
        values = chan[:, pl.ds(base, samp + TAIL)]
        a = window_sum(values)[:, :samp] / WIN
        q = window_sum(values * values)[:, :samp] / WIN
        inverse = 1.0 / jnp.sqrt(jnp.maximum(q - a * a, 0.0) + EPSILON)
        g = weight * inverse
        gain[...] = jnp.concatenate(
            [g] * SHIFTS + [jnp.zeros((LANES - rows_in, samp), jnp.float32)], axis=0
        ).T

        def fill(r, inner):
            at = pl.multiple_of(r * sub, sub)
            scaled = gain[pl.ds(at, sub), :]
            for j in range(steps):
                x = rows[pl.ds(base + at + j * SHIFTS, sub), :]
                win[pl.ds(at, sub), pl.ds(j * LANES, LANES)] = (x * scaled).astype(jnp.bfloat16)
            return inner

        lax.fori_loop(0, samp // sub, fill, 0)
        product = lax.dot_general(
            win[...], tpl[...], (((1,), (1,)), ((), ())), preferred_element_type=jnp.float32
        )
        slot = lax.rem(i, 2) * (GROUP // 2) + i // 2
        out_ref[slot] = product.T[:count] * factor
        return carry

    lax.fori_loop(0, GROUP, stack, 0)


def correlate(everyone, start, weight, plane, n, samp, factor):
    parts = everyone.shape[1] // 2
    count = start.shape[0]
    total = n * samp
    deep = WIN // SHIFTS * LANES
    return pl.pallas_call(
        functools.partial(correlate_kernel, n, samp, factor),
        out_shape=jax.ShapeDtypeStruct((GROUP, count, samp), jnp.float32),
        in_specs=[SMEM, SMEM, VMEM, VMEM],
        out_specs=VMEM,
        scratch_shapes=[
            pltpu.VMEM((parts, total + TAIL), jnp.float32),
            pltpu.VMEM((total + TAIL, LANES), jnp.float32),
            pltpu.VMEM((24 * count, LANES), jnp.float32),
            pltpu.VMEM((LANES, deep), jnp.bfloat16),
            pltpu.VMEM((samp, LANES), jnp.float32),
            pltpu.VMEM((samp, deep), jnp.bfloat16),
        ],
        compiler_params=pltpu.CompilerParams(vmem_limit_bytes=48 * 1024 * 1024),
    )(plane, start, everyone, weight)


def reduce_kernel(part_ref, out_ref, pair, far, mid, pair_send, pair_recv, far_send, far_recv):
    me = lax.axis_index("tm")
    chips = GROUP // 2
    base = (me // GROUP) * GROUP
    place = lax.rem(me, GROUP)
    core, chip = lax.rem(place, 2), place // 2
    other = base + chip * 2 + (1 - core)
    barrier = pltpu.get_barrier_semaphore()
    pl.semaphore_signal(barrier, inc=1, device_id={"tm": other}, device_id_type=MESH)
    for d in range(1, chips):
        to = base + lax.rem(chip + d, chips) * 2 + core
        pl.semaphore_signal(barrier, inc=1, device_id={"tm": to}, device_id_type=MESH)
    pl.semaphore_wait(barrier, chips)
    first = []
    for d in (2, 1, 3, 0):
        slot = lax.rem(chip + d, chips)
        copy = pltpu.make_async_remote_copy(
            src_ref=part_ref.at[1 - core, slot],
            dst_ref=pair.at[d],
            send_sem=pair_send.at[d],
            recv_sem=pair_recv.at[d],
            device_id={"tm": other},
            device_id_type=MESH,
        )
        copy.start()
        first.append((d, slot, copy))
    second = []
    for d, slot, copy in first:
        copy.wait_recv()
        if d:
            mid[d] = part_ref[core, slot] + pair[d]
            far_copy = pltpu.make_async_remote_copy(
                src_ref=mid.at[d],
                dst_ref=far.at[d],
                send_sem=far_send.at[d],
                recv_sem=far_recv.at[d],
                device_id={"tm": base + slot * 2 + core},
                device_id_type=MESH,
            )
            far_copy.start()
            second.append((d, far_copy))
        else:
            out_ref[...] = part_ref[core, slot] + pair[d]
    for d, far_copy in second:
        far_copy.wait_recv()
        out_ref[...] += far[d]
    for d, slot, copy in first:
        copy.wait_send()
    for d, far_copy in second:
        far_copy.wait_send()


def reduce_group(partial):
    chips = GROUP // 2
    shape = partial.shape[1:]
    block = pltpu.VMEM((chips,) + shape, jnp.float32)
    return pl.pallas_call(
        reduce_kernel,
        out_shape=jax.ShapeDtypeStruct(shape, jnp.float32),
        in_specs=[VMEM],
        out_specs=VMEM,
        scratch_shapes=[block, block, block]
        + [pltpu.SemaphoreType.DMA((chips,)) for unused in range(4)],
        compiler_params=pltpu.CompilerParams(
            collective_id=1, has_side_effects=True, vmem_limit_bytes=32 * 1024 * 1024
        ),
    )(partial.reshape((2, chips) + shape))


def body(record, owner, offset, station, valid):
    ch_dev, samp = record.shape
    n = lax.axis_size("tm")
    me = lax.axis_index("tm")
    parts = ch_dev // GROUP
    mine = record.astype(jnp.bfloat16).reshape(GROUP, parts, 2, samp // 2)
    mine = mine.transpose(0, 2, 1, 3).reshape(GROUP, 2 * parts, samp // 2)
    everyone = exchange(mine, n)

    stations = ch_dev * lax.axis_size("sta") // 3
    station_table = (station[:, None] == jnp.arange(stations, dtype=jnp.int32)[None, :]).astype(
        jnp.float32
    )
    present = valid.astype(jnp.float32)
    counts = lax.psum(jnp.sum(present[:, None] * station_table, axis=0), "sta")
    own_counts = jnp.sum(station_table * counts[None, :], axis=1)
    weight = present / jnp.maximum(own_counts, 1.0)
    own_weight = lax.dynamic_slice_in_dim(weight, lax.rem(me, GROUP) * parts, parts, 0)

    start = owner[:, 0] * samp + offset
    plane = (me // GROUP).reshape(1)
    factor = 1.0 / math.sqrt(stations)
    partial = correlate(everyone, start, own_weight[:, None], plane, n, samp, factor)
    stack = reduce_group(partial)
    stack = stack.reshape(NSTEP, TPL_STEP, samp)
    return lax.psum_scatter(stack, "sta", scatter_dimension=1, tiled=True)


def solution(mesh):
    placed = (P("sta", "tm"), P(), P(), P("sta"), P("sta"))
    return jax.shard_map(
        body, mesh=mesh, in_specs=placed, out_specs=P(None, "sta", "tm"), check_vma=False
    )
```

time: 564 us -> 69.9 us (0.12)
  the two profiles are of different devices: /device:TPU:0 before, /device:TPU:9 now
where the time goes in v1:
time: 69.9 us; the launch traced here: 69.7 us
  Pallas kernels  64.1 us (92%)
  other arithmetic  4.63 us (7%)
  local copies, waits for them, and re-layouts  0.92 us (1%)
    pallas_call x1, Pallas kernels, correlate(): pl.pallas_call(functools.partial(correlate_kernel, n, samp, factor), out_...  26.1 us
    pallas_call x1, Pallas kernels, exchange(): pl.pallas_call(functools.partial(exchange_kernel, n), out_shape=jax.Shape...  22.4 us
    pallas_call x1, Pallas kernels, reduce_group(): pl.pallas_call(reduce_kernel, out_shape=jax.ShapeDtypeStruct(shape, jnp.f...  15.6 us

profile of v1, /device:TPU:9, one launch (start us, length us, event | category | flops | bytes accessed | tf_op | source)
XLA Modules:
  0.0 69.7 jit_solution(16454131316487080253)
XLA Ops:
  0.0 0.7 bitcast_add_fusion.start_ref
  0.7 0.7 convert_element_type.8
  1.4 0.8 %select_reduce_fusion.1 = f32[64]{0:T(128)S(1)} fusion(f32[192]{0:T(256)S(1)} %convert_element_type.8, s32[192]{0:T(256)} %param.8), kind=kLoop, calls=%fused_computation.1 | loop fusion | flops 36800 | bytes 1792 | tf_op jit(solution)/shard_map/reduce_sum | solution.py:305
  2.1 0.8 %select_reduce_fusion = f32[192]{0:T(256)S(1)} fusion(f32[64]{0:T(128)S(1)} %select_reduce_fusion.1, s32[192]{0:T(256)} %param.8), kind=kLoop, calls=%fused_computation | loop fusion | flops 36672 | bytes 1792 | tf_op jit(solution)/shard_map/reduce_sum | solution.py:306
  2.9 0.7 maximum_divide_fusion
  3.6 0.1 dynamic-slice_bitcast_fusion
  3.7 0.1 copy.9.weight_ref
  3.8 1.0 %convert_element_type.7 = bf16[192,512]{1,0:T(8,128)(2,1)S(1)} convert(f32[192,512]{1,0:T(8,128)} %param.5) | non-fusion elementwise | flops 98304 | bytes 589824 | tf_op jit(solution)/shard_map/convert_element_type | solution.py:296
  4.8 0.1 reshape.21
  4.9 22.4 %shard_map.55.all_ref = bf16[32,48,256]{2,1,0:T(8,128)(2,1)S(1)} custom-call(bf16[8,48,256]{2,1,0:T(8,128)(2,1)S(1)} %bitcast.12), custom_call_target="tpu_custom_call" | custom-call | tf_op jit(solution)/shard_map/pallas_call | solution.py:72
  27.3 26.1 %shard_map.56 = f32[8,96,512]{2,1,0:T(8,128)S(1)} custom-call(s32[1]{0:T(128)} %bitcast.plane_ref, s32[96]{0:T(128)S(1)} %bitcast_add_fusion.start_ref, bf16[32,48,256]{2,1,0:T(8,128)(2,1)S(1)} %shard_map.55.all_ref, f32[24,1]{1,0:T(8,128)S(1)} %copy.9.weight_ref), custom_call_target="tpu_custom_call" | custom-call | tf_op jit(solution)/shard_map/pallas_call | solution.py:205
  53.4 15.6 %shard_map.57 = f32[96,512]{1,0:T(8,128)S(1)} custom-call(f32[2,4,96,512]{3,2,1,0:T(8,128)S(1)} %bitcast.10), custom_call_target="tpu_custom_call" | custom-call | tf_op jit(solution)/shard_map/pallas_call | solution.py:278
  69.0 0.7 copy.11
  (1 shorter events, 0.0 us)

commit v2 on v0

v2 whole, which is shorter than its diff:
```python
import functools
import math

import jax
import jax.numpy as jnp
from jax import lax
from jax.experimental import pallas as pl
from jax.experimental.pallas import tpu as pltpu
from jax.sharding import PartitionSpec as P

WIN = 100
TPL_STEP = 32
NSTEP = 3
EPSILON = 1e-05
GROUP = 8
SHIFTS = 5
LANES = 128
TAIL = 256
MESH = pl.DeviceIdType.MESH
VMEM = pl.BlockSpec(memory_space=pltpu.VMEM)
SMEM = pl.BlockSpec(memory_space=pltpu.SMEM)


def ahead(array, by):
    return pltpu.roll(array, array.shape[1] - by, 1) if by else array


def window_sum(x):
    two = x + ahead(x, 1)
    four = two + ahead(two, 2)
    eight = four + ahead(four, 4)
    sixteen = eight + ahead(eight, 8)
    half = sixteen + ahead(sixteen, 16)
    full = half + ahead(half, 32)
    return full + ahead(half, 64) + ahead(four, 96)


def fused_kernel(
    n, samp, factor, owner_ref, offset_ref, record_ref, station_ref, valid_ref, out_ref,
    mine, everyone, chan, rows, raw, tpl, gain, win, part, pair, from_a, from_b,
    send_sem, recv_sem, own_sem, pair_send, pair_recv, a_send, a_recv, b_send, b_recv,
):
    me = lax.axis_index("tm")
    plane = me // GROUP
    base = plane * GROUP
    place = lax.rem(me, GROUP)
    parts = mine.shape[1] // 2
    half = samp // 2
    rows_in = SHIFTS * parts
    steps = WIN // SHIFTS
    count = owner_ref.shape[0]
    total = n * samp

    def remote(src, dst, send, recv, to):
        return pltpu.make_async_remote_copy(
            src_ref=src, dst_ref=dst, send_sem=send, recv_sem=recv,
            device_id={"tm": to}, device_id_type=MESH,
        )

    barrier = pltpu.get_barrier_semaphore()

    def greet(d, carry):
        pl.semaphore_signal(
            barrier, inc=1, device_id={"tm": lax.rem(me + d, n)}, device_id_type=MESH
        )
        return carry

    lax.fori_loop(1, n, greet, 0)
    for g in range(GROUP):
        block = record_ref[pl.ds(g * parts, parts), :]
        mine[g] = jnp.concatenate([block[:, :half], block[:, half:]], axis=0).astype(jnp.bfloat16)
    own = pltpu.make_async_copy(mine.at[place], everyone.at[me], own_sem)
    own.start()
    pl.semaphore_wait(barrier, n - 1)

    def target(d):
        return lax.rem(base + (d // GROUP) * GROUP + lax.rem(place + d, GROUP), n)

    def send(d, carry):
        to = target(d)
        remote(
            mine.at[lax.rem(to, GROUP)], everyone.at[me], send_sem.at[d], recv_sem.at[me], to
        ).start()
        return carry

    lax.fori_loop(1, n, send, 0)

    wide = station_ref.shape[1]
    lane = lax.broadcasted_iota(jnp.int32, (parts, wide), 1)
    row = lax.broadcasted_iota(jnp.int32, (parts, wide), 0)
    first_channel = lax.axis_index("sta") * (GROUP * parts) + place * parts
    here = lane == row + first_channel
    stations = station_ref[...].astype(jnp.float32)
    present = valid_ref[...].astype(jnp.float32)
    own_station = jnp.sum(jnp.where(here, stations, 0.0), axis=1, keepdims=True)
    own_valid = jnp.sum(jnp.where(here, present, 0.0), axis=1, keepdims=True)
    counts = jnp.sum(jnp.where(stations == own_station, present, 0.0), axis=1, keepdims=True)
    weight = own_valid / jnp.maximum(counts, 1.0)

    chan[:, pl.ds(total, TAIL)] = jnp.zeros((parts, TAIL), jnp.float32)

    def spread(j):
        block = everyone[j].astype(jnp.float32)
        chan[:, pl.ds(pl.multiple_of(j * samp, samp), half)] = block[:parts]
        chan[:, pl.ds(pl.multiple_of(j * samp + half, half), half)] = block[parts:]

    def arrived(j):
        remote(mine.at[0], everyone.at[j], send_sem.at[0], recv_sem.at[j], j).wait_recv()

    def turn(at, length):
        values = chan[:, pl.ds(at, length + LANES)]
        pieces = [ahead(values, k)[:, :length] for k in range(SHIFTS)]
        pieces.append(jnp.zeros((LANES - rows_in, length), jnp.float32))
        rows[pl.ds(at, length), :] = jnp.concatenate(pieces, axis=0).T

    own.wait()
    spread(me)

    def take_plane(d, carry):
        source = base + lax.rem(place + d, GROUP)
        arrived(source)
        spread(source)
        return carry

    lax.fori_loop(1, GROUP, take_plane, 0)
    after = lax.rem(base + GROUP, n)
    arrived(after)
    spread(after)
    first = pl.multiple_of(base * samp, samp)

    def turn_own(i, carry):
        turn(pl.multiple_of(first + i * samp, samp), samp)
        return carry

    lax.fori_loop(0, GROUP, turn_own, 0)
    turn(pl.multiple_of(first + GROUP * samp, samp), LANES)
    sub = 64

    def window(i, carry):
        at_block = pl.multiple_of(first + i * samp, samp)
        values = chan[:, pl.ds(at_block, samp + LANES)]
        a = window_sum(values)[:, :samp] / WIN
        q = window_sum(values * values)[:, :samp] / WIN
        inverse = 1.0 / jnp.sqrt(jnp.maximum(q - a * a, 0.0) + EPSILON)
        g = weight * inverse
        gain[...] = jnp.concatenate(
            [g] * SHIFTS + [jnp.zeros((LANES - rows_in, samp), jnp.float32)], axis=0
        ).T

        def fill(r, inner):
            at = pl.multiple_of(r * sub, sub)
            scaled = gain[pl.ds(at, sub), :]
            for j in range(steps):
                x = rows[pl.ds(at_block + at + j * SHIFTS, sub), :]
                win[i, pl.ds(at, sub), pl.ds(j * LANES, LANES)] = (x * scaled).astype(jnp.bfloat16)
            return inner

        lax.fori_loop(0, samp // sub, fill, 0)
        return carry

    lax.fori_loop(0, GROUP, window, 0)

    def take_far(e, carry):
        source = lax.rem(base + e, n)
        arrived(source)
        spread(source)
        turn(pl.multiple_of(lax.rem(base + e - 1, n) * samp, samp), samp)
        return carry

    lax.fori_loop(GROUP + 1, n, take_far, 0)
    turn(pl.multiple_of(lax.rem(base + n - 1, n) * samp, samp), samp)
    rows[pl.ds(total, LANES), :] = jnp.zeros((LANES, LANES), jnp.float32)

    def pick(t, carry):
        start = owner_ref[t] * samp + offset_ref[t]
        raw[pl.ds(t, 24, stride=count), :] = rows[pl.ds(start, 24, stride=SHIFTS), :]
        return carry

    lax.fori_loop(0, count, pick, 0)
    lane_a = lax.broadcasted_iota(jnp.int32, (LANES, LANES), 0)
    lane_b = lax.broadcasted_iota(jnp.int32, (LANES, LANES), 1)
    same = (lax.rem(lane_a, parts) == lax.rem(lane_b, parts)) & (
        (lane_a < rows_in) & (lane_b < rows_in)
    )
    fold = jnp.where(same, 1.0, 0.0).astype(jnp.float32)

    def folded(x):
        return jnp.dot(
            x, fold, precision=lax.Precision.HIGHEST, preferred_element_type=jnp.float32
        )

    sums = raw[pl.ds(0, count), :]
    for j in range(1, steps):
        sums = sums + raw[pl.ds(j * count, count), :]
    mean = folded(sums) / WIN
    square = jnp.zeros_like(mean)
    for j in range(steps):
        centred = raw[pl.ds(j * count, count), :] - mean
        square = square + centred * centred
    spread_of = jnp.sqrt(folded(square) / WIN + EPSILON)
    scale = 1.0 / (WIN * spread_of)
    for j in range(steps):
        value = (raw[pl.ds(j * count, count), :] - mean) * scale
        tpl[pl.ds(0, count), pl.ds(j * LANES, LANES)] = value.astype(jnp.bfloat16)
    tpl[pl.ds(count, LANES - count), :] = jnp.zeros(
        (LANES - count, tpl.shape[1]), jnp.bfloat16
    )

    core, x, y = lax.rem(place, 2), lax.rem(place // 2, 2), place // 4
    xa, ya = x + (1 - 2 * x) * (1 - core), y + (1 - 2 * y) * core
    xb, yb = x + (1 - 2 * x) * core, y + (1 - 2 * y) * (1 - core)
    own_chip, chip_a, chip_b = y * 2 + x, ya * 2 + xa, yb * 2 + xb
    diagonal = (1 - y) * 2 + (1 - x)
    mine_order = [diagonal, chip_a, chip_b, own_chip]
    pair_order = [diagonal, chip_b, chip_a, own_chip]
    to_pair = base + own_chip * 2 + (1 - core)
    to_a = base + chip_a * 2 + core
    to_b = base + chip_b * 2 + core
    pair_copies, a_copies, b_copies = [], [], []

    def join(q):
        pair_copies[q].wait_recv()
        part[q, 1] += pair[q]

    for q in range(4):
        block_pair = pair_order[q] * 2 + (1 - core)
        block_mine = mine_order[q] * 2 + core

        def multiply(h, carry, q=q, block_pair=block_pair, block_mine=block_mine):
            block = block_pair + h * (block_mine - block_pair)
            product = lax.dot_general(
                win[block], tpl[...], (((1,), (1,)), ((), ())),
                preferred_element_type=jnp.float32,
            )
            part[q, h] = product.T[:count] * factor
            return carry

        lax.fori_loop(0, 2, multiply, 0)
        copy = remote(part.at[q, 0], pair.at[q], pair_send.at[q], pair_recv.at[q], to_pair)
        copy.start()
        pair_copies.append(copy)
        if q:
            join(q - 1)
        if q in (1, 2):
            copy = remote(
                part.at[q - 1, 1], from_a.at[q - 1], a_send.at[q - 1], a_recv.at[q - 1], to_a
            )
            copy.start()
            a_copies.append(copy)
        if q == 3:
            a_copies[0].wait_recv()
            part[2, 1] += from_a[0]
            copy = remote(part.at[2, 1], from_b, b_send, b_recv, to_b)
            copy.start()
            b_copies.append(copy)
    join(3)
    a_copies[1].wait_recv()
    part[3, 1] += from_a[1]
    b_copies[0].wait_recv()
    out_ref[...] = part[3, 1] + from_b[...]
    for copy in pair_copies + a_copies + b_copies:
        copy.wait_send()

    def sent(d, carry):
        remote(
            mine.at[0], everyone.at[me], send_sem.at[d], recv_sem.at[me], target(d)
        ).wait_send()
        return carry

    lax.fori_loop(1, n, sent, 0)


def body(record, owner, offset, station, valid):
    ch_dev, samp = record.shape
    n = lax.axis_size("tm")
    parts = ch_dev // GROUP
    count = offset.shape[0]
    total = n * samp
    deep = WIN // SHIFTS * LANES
    stations = ch_dev * lax.axis_size("sta") // 3
    station = lax.all_gather(station, "sta", axis=0, tiled=True)
    valid = lax.all_gather(valid, "sta", axis=0, tiled=True)
    dma = pltpu.SemaphoreType.DMA
    f32, bf16 = jnp.float32, jnp.bfloat16
    stack = pl.pallas_call(
        functools.partial(fused_kernel, n, samp, 1.0 / math.sqrt(stations)),
        out_shape=jax.ShapeDtypeStruct((count, samp), f32),
        in_specs=[SMEM, SMEM, VMEM, VMEM, VMEM],
        out_specs=VMEM,
        scratch_shapes=[
            pltpu.VMEM((GROUP, 2 * parts, samp // 2), bf16),
            pltpu.VMEM((n, 2 * parts, samp // 2), bf16),
            pltpu.VMEM((parts, total + TAIL), f32),
            pltpu.VMEM((total + LANES, LANES), f32),
            pltpu.VMEM((24 * count, LANES), f32),
            pltpu.VMEM((LANES, deep), bf16),
            pltpu.VMEM((samp, LANES), f32),
            pltpu.VMEM((GROUP, samp, deep), bf16),
            pltpu.VMEM((4, 2, count, samp), f32),
            pltpu.VMEM((4, count, samp), f32),
            pltpu.VMEM((2, count, samp), f32),
            pltpu.VMEM((count, samp), f32),
            dma((n,)), dma((n,)), dma,
            dma((4,)), dma((4,)), dma((2,)), dma((2,)), dma, dma,
        ],
        compiler_params=pltpu.CompilerParams(
            collective_id=0, has_side_effects=True, vmem_limit_bytes=56 * 1024 * 1024
        ),
    )(owner.reshape(-1), offset, record, station[None, :], valid[None, :])
    stack = stack.reshape(NSTEP, TPL_STEP, samp)
    return lax.psum_scatter(stack, "sta", scatter_dimension=1, tiled=True)


def solution(mesh):
    placed = (P("sta", "tm"), P(), P(), P("sta"), P("sta"))
    return jax.shard_map(
        body, mesh=mesh, in_specs=placed, out_specs=P(None, "sta", "tm"), check_vma=False
    )
```

time: 564 us -> 59.7 us (0.11)
  the two profiles are of different devices: /device:TPU:0 before, /device:TPU:8 now
where the time goes in v2:
time: 59.7 us; the launch traced here: 59.5 us
  Pallas kernels  57.9 us (97%)
  local copies, waits for them, and re-layouts  1.62 us (3%)
    pallas_call x1, Pallas kernels, body(): pl.pallas_call(functools.partial(fused_kernel, n, samp, 1.0 / math.sqrt(s...  57.9 us
    unnamed x1, local copies, waits for them, and re-layouts  1.62 us

profile of v2, /device:TPU:8, one launch (start us, length us, event | category | flops | bytes accessed | tf_op | source)
XLA Modules:
  0.0 59.5 jit_solution(8373032041878578137)
XLA Ops:
  0.0 57.9 %shard_map.55 = f32[96,512]{1,0:T(8,128)} custom-call(s32[96]{0:T(128)} %bitcast.7, s32[96]{0:T(128)} %offset_ref.1, f32[192,512]{1,0:T(8,128)} %record_ref.1, s32[1,192]{1,0:T(1,128)} %bitcast.5, s32[1,192]{1,0:T(1,128)} %bitcast.6), custom_call_target="tpu_custom_call" | custom-call | tf_op jit(solution)/shard_map/pallas_call | solution.py:285
  57.9 1.6 %copy.7 = f32[3,32,512]{2,1,0:T(8,128)} copy(f32[3,32,512]{2,1,0:T(8,128)} %bitcast.4) | data formatting | bytes 393216

commit v3 on v2

--- a/solution.py
+++ b/solution.py
@@ -37,7 +37,7 @@
 
 def fused_kernel(
     n, samp, factor, owner_ref, offset_ref, record_ref, station_ref, valid_ref, out_ref,
-    mine, everyone, chan, rows, raw, tpl, gain, win, part, pair, from_a, from_b,
+    mine, everyone, eye, chan, rows, raw, tpl, gain, win, part, pair, from_a, from_b,
     send_sem, recv_sem, own_sem, pair_send, pair_recv, a_send, a_recv, b_send, b_recv,
 ):
     me = lax.axis_index("tm")
@@ -74,7 +74,7 @@
     pl.semaphore_wait(barrier, n - 1)
 
     def target(d):
-        return lax.rem(base + (d // GROUP) * GROUP + lax.rem(place + d, GROUP), n)
+        return lax.rem(base + n - (d // GROUP) * GROUP + lax.rem(place + d, GROUP), n)
 
     def send(d, carry):
         to = target(d)
@@ -97,6 +97,10 @@
     counts = jnp.sum(jnp.where(stations == own_station, present, 0.0), axis=1, keepdims=True)
     weight = own_valid / jnp.maximum(counts, 1.0)
 
+    eye[...] = jnp.where(
+        lax.broadcasted_iota(jnp.int32, eye.shape, 0) == lax.broadcasted_iota(jnp.int32, eye.shape, 1),
+        1.0, 0.0,
+    ).astype(jnp.bfloat16)
     chan[:, pl.ds(total, TAIL)] = jnp.zeros((parts, TAIL), jnp.float32)
 
     def spread(j):
@@ -111,7 +115,13 @@
         values = chan[:, pl.ds(at, length + LANES)]
         pieces = [ahead(values, k)[:, :length] for k in range(SHIFTS)]
         pieces.append(jnp.zeros((LANES - rows_in, length), jnp.float32))
-        rows[pl.ds(at, length), :] = jnp.concatenate(pieces, axis=0).T
+        wide_rows = jnp.concatenate(pieces, axis=0).astype(jnp.bfloat16)
+        for cut in range(0, length, 2 * LANES):
+            size = min(2 * LANES, length - cut)
+            rows[pl.ds(at + cut, size), :] = lax.dot_general(
+                eye[pl.ds(0, size), pl.ds(0, size)], wide_rows[:, cut : cut + size],
+                (((1,), (1,)), ((), ())), preferred_element_type=jnp.float32,
+            )
 
     own.wait()
     spread(me)
@@ -123,17 +133,13 @@
         return carry
 
     lax.fori_loop(1, GROUP, take_plane, 0)
-    after = lax.rem(base + GROUP, n)
-    arrived(after)
-    spread(after)
     first = pl.multiple_of(base * samp, samp)
 
     def turn_own(i, carry):
         turn(pl.multiple_of(first + i * samp, samp), samp)
         return carry
 
-    lax.fori_loop(0, GROUP, turn_own, 0)
-    turn(pl.multiple_of(first + GROUP * samp, samp), LANES)
+    lax.fori_loop(0, GROUP - 1, turn_own, 0)
     sub = 64
 
     def window(i, carry):
@@ -158,7 +164,13 @@
         lax.fori_loop(0, samp // sub, fill, 0)
         return carry
 
-    lax.fori_loop(0, GROUP, window, 0)
+    lax.fori_loop(0, GROUP - 2, window, 0)
+    after = lax.rem(base + GROUP, n)
+    arrived(after)
+    spread(after)
+    turn_own(GROUP - 1, 0)
+    turn(pl.multiple_of(first + GROUP * samp, samp), LANES)
+    lax.fori_loop(GROUP - 2, GROUP, window, 0)
 
     def take_far(e, carry):
         source = lax.rem(base + e, n)
@@ -171,12 +183,16 @@
     turn(pl.multiple_of(lax.rem(base + n - 1, n) * samp, samp), samp)
     rows[pl.ds(total, LANES), :] = jnp.zeros((LANES, LANES), jnp.float32)
 
-    def pick(t, carry):
-        start = owner_ref[t] * samp + offset_ref[t]
-        raw[pl.ds(t, 24, stride=count), :] = rows[pl.ds(start, 24, stride=SHIFTS), :]
-        return carry
-
-    lax.fori_loop(0, count, pick, 0)
+    def pick(b, carry):
+        found = []
+        for t in range(8):
+            start = owner_ref[b * 8 + t] * samp + offset_ref[b * 8 + t]
+            found.append(rows[pl.ds(start, 24, stride=SHIFTS), :])
+        for t in range(8):
+            raw[pl.ds(b * 8 + t, 24, stride=count), :] = found[t]
+        return carry
+
+    lax.fori_loop(0, count // 8, pick, 0)
     lane_a = lax.broadcasted_iota(jnp.int32, (LANES, LANES), 0)
     lane_b = lax.broadcasted_iota(jnp.int32, (LANES, LANES), 1)
     same = (lax.rem(lane_a, parts) == lax.rem(lane_b, parts)) & (
@@ -290,6 +306,7 @@
         scratch_shapes=[
             pltpu.VMEM((GROUP, 2 * parts, samp // 2), bf16),
             pltpu.VMEM((n, 2 * parts, samp // 2), bf16),
+            pltpu.VMEM((2 * LANES, 2 * LANES), bf16),
             pltpu.VMEM((parts, total + TAIL), f32),
             pltpu.VMEM((total + LANES, LANES), f32),
             pltpu.VMEM((24 * count, LANES), f32),

time: 59.7 us -> 50.7 us (0.85)
  the two profiles are of different devices: /device:TPU:8 before, /device:TPU:0 now
where the time goes in v3:
time: 50.7 us; the launch traced here: 50.6 us
  Pallas kernels  49 us (97%)
  local copies, waits for them, and re-layouts  1.62 us (3%)
    pallas_call x1, Pallas kernels, body(): pl.pallas_call(functools.partial(fused_kernel, n, samp, 1.0 / math.sqrt(s...  49 us
    unnamed x1, local copies, waits for them, and re-layouts  1.62 us

profile of v3, /device:TPU:0, one launch (start us, length us, event | category | flops | bytes accessed | tf_op | source)
XLA Modules:
  0.0 50.6 jit_solution(11364563503153210258)
XLA Ops:
  0.0 49.0 %shard_map.55 = f32[96,512]{1,0:T(8,128)} custom-call(s32[96]{0:T(128)} %bitcast.7, s32[96]{0:T(128)} %offset_ref.1, f32[192,512]{1,0:T(8,128)} %record_ref.1, s32[1,192]{1,0:T(1,128)} %bitcast.5, s32[1,192]{1,0:T(1,128)} %bitcast.6), custom_call_target="tpu_custom_call" | custom-call | tf_op jit(solution)/shard_map/pallas_call | solution.py:301
  49.0 1.6 %copy.7 = f32[3,32,512]{2,1,0:T(8,128)} copy(f32[3,32,512]{2,1,0:T(8,128)} %bitcast.4) | data formatting | bytes 393216

commit v4 on v3

--- a/solution.py
+++ b/solution.py
@@ -135,52 +135,59 @@
     lax.fori_loop(1, GROUP, take_plane, 0)
     first = pl.multiple_of(base * samp, samp)
 
-    def turn_own(i, carry):
+    for i in range(GROUP - 1):
         turn(pl.multiple_of(first + i * samp, samp), samp)
-        return carry
-
-    lax.fori_loop(0, GROUP - 1, turn_own, 0)
     sub = 64
 
-    def window(i, carry):
-        at_block = pl.multiple_of(first + i * samp, samp)
-        values = chan[:, pl.ds(at_block, samp + LANES)]
-        a = window_sum(values)[:, :samp] / WIN
-        q = window_sum(values * values)[:, :samp] / WIN
+    def gains(at, length):
+        values = chan[:, pl.ds(at, length + LANES)]
+        a = window_sum(values)[:, :length] / WIN
+        q = window_sum(values * values)[:, :length] / WIN
         inverse = 1.0 / jnp.sqrt(jnp.maximum(q - a * a, 0.0) + EPSILON)
         g = weight * inverse
-        gain[...] = jnp.concatenate(
-            [g] * SHIFTS + [jnp.zeros((LANES - rows_in, samp), jnp.float32)], axis=0
+        zeros = jnp.zeros((LANES - rows_in, length), jnp.float32)
+        gain[pl.ds(pl.multiple_of(at - first, samp), length), :] = jnp.concatenate(
+            [g] * SHIFTS + [zeros], axis=0
         ).T
 
-        def fill(r, inner):
-            at = pl.multiple_of(r * sub, sub)
-            scaled = gain[pl.ds(at, sub), :]
-            for j in range(steps):
-                x = rows[pl.ds(at_block + at + j * SHIFTS, sub), :]
-                win[i, pl.ds(at, sub), pl.ds(j * LANES, LANES)] = (x * scaled).astype(jnp.bfloat16)
-            return inner
-
-        lax.fori_loop(0, samp // sub, fill, 0)
-        return carry
-
-    lax.fori_loop(0, GROUP - 2, window, 0)
+    def gains_two(i, carry):
+        gains(pl.multiple_of(first + i * (2 * samp), samp), 2 * samp)
+        return carry
+
+    def fill(r, carry):
+        at = pl.multiple_of(r * sub, sub)
+        scaled = gain[pl.ds(at, sub), :]
+        for j in range(steps):
+            x = rows[pl.ds(first + at + j * SHIFTS, sub), :]
+            win[pl.ds(at, sub), pl.ds(j * LANES, LANES)] = (x * scaled).astype(jnp.bfloat16)
+        return carry
+
+    early = (GROUP - 2) * samp // sub
+    lax.fori_loop(0, GROUP // 2 - 1, gains_two, 0)
+    lax.fori_loop(0, early, fill, 0)
     after = lax.rem(base + GROUP, n)
     arrived(after)
     spread(after)
-    turn_own(GROUP - 1, 0)
+    turn(pl.multiple_of(first + (GROUP - 1) * samp, samp), samp)
     turn(pl.multiple_of(first + GROUP * samp, samp), LANES)
-    lax.fori_loop(GROUP - 2, GROUP, window, 0)
-
-    def take_far(e, carry):
-        source = lax.rem(base + e, n)
-        arrived(source)
-        spread(source)
-        turn(pl.multiple_of(lax.rem(base + e - 1, n) * samp, samp), samp)
-        return carry
-
-    lax.fori_loop(GROUP + 1, n, take_far, 0)
-    turn(pl.multiple_of(lax.rem(base + n - 1, n) * samp, samp), samp)
+    gains_two(GROUP // 2 - 1, 0)
+    lax.fori_loop(early, GROUP * samp // sub, fill, 0)
+
+    def take_far(e, blocks):
+        for d in range(blocks):
+            source = lax.rem(base + e + d, n)
+            arrived(source)
+            spread(source)
+        for d in range(4):
+            turn(pl.multiple_of(lax.rem(base + e + d - 1, n) * samp, samp), samp)
+
+    def take_four(i, carry):
+        take_far(GROUP + 1 + i * 4, 4)
+        return carry
+
+    far = n - GROUP - 1
+    lax.fori_loop(0, far // 4, take_four, 0)
+    take_far(n - far % 4, far % 4)
     rows[pl.ds(total, LANES), :] = jnp.zeros((LANES, LANES), jnp.float32)
 
     def pick(b, carry):
@@ -242,16 +249,12 @@
         block_pair = pair_order[q] * 2 + (1 - core)
         block_mine = mine_order[q] * 2 + core
 
-        def multiply(h, carry, q=q, block_pair=block_pair, block_mine=block_mine):
-            block = block_pair + h * (block_mine - block_pair)
+        for h, block in ((0, block_pair), (1, block_mine)):
             product = lax.dot_general(
-                win[block], tpl[...], (((1,), (1,)), ((), ())),
-                preferred_element_type=jnp.float32,
+                win[pl.ds(pl.multiple_of(block * samp, samp), samp), :], tpl[...],
+                (((1,), (1,)), ((), ())), preferred_element_type=jnp.float32,
             )
             part[q, h] = product.T[:count] * factor
-            return carry
-
-        lax.fori_loop(0, 2, multiply, 0)
         copy = remote(part.at[q, 0], pair.at[q], pair_send.at[q], pair_recv.at[q], to_pair)
         copy.start()
         pair_copies.append(copy)
@@ -311,8 +314,8 @@
             pltpu.VMEM((total + LANES, LANES), f32),
             pltpu.VMEM((24 * count, LANES), f32),
             pltpu.VMEM((LANES, deep), bf16),
-            pltpu.VMEM((samp, LANES), f32),
-            pltpu.VMEM((GROUP, samp, deep), bf16),
+            pltpu.VMEM((GROUP * samp, LANES), f32),
+            pltpu.VMEM((GROUP * samp, deep), bf16),
             pltpu.VMEM((4, 2, count, samp), f32),
             pltpu.VMEM((4, count, samp), f32),
             pltpu.VMEM((2, count, samp), f32),

time: 50.7 us -> 47.5 us (0.937)
  Pallas kernels: 49 us -> 45.7 us
    pallas_call x1, Pallas kernels: 49 us -> 45.7 us  [body(): pl.pallas_call(functools.partial(fused_kernel, n, samp, 1.0 / math.sqrt(s...]
where the time goes in v4:
time: 47.5 us; the launch traced here: 47.4 us
  Pallas kernels  45.7 us (96%)
  local copies, waits for them, and re-layouts  1.62 us (3%)
    pallas_call x1, Pallas kernels, body(): pl.pallas_call(functools.partial(fused_kernel, n, samp, 1.0 / math.sqrt(s...  45.7 us
    unnamed x1, local copies, waits for them, and re-layouts  1.62 us

profile of v4, /device:TPU:0, one launch (start us, length us, event | category | flops | bytes accessed | tf_op | source)
XLA Modules:
  0.0 47.4 jit_solution(2661161411996253676)
XLA Ops:
  0.0 45.7 %shard_map.55 = f32[96,512]{1,0:T(8,128)} custom-call(s32[96]{0:T(128)} %bitcast.7, s32[96]{0:T(128)} %offset_ref.1, f32[192,512]{1,0:T(8,128)} %record_ref.1, s32[1,192]{1,0:T(1,128)} %bitcast.5, s32[1,192]{1,0:T(1,128)} %bitcast.6), custom_call_target="tpu_custom_call" | custom-call | tf_op jit(solution)/shard_map/pallas_call | solution.py:304
  45.7 1.6 %copy.7 = f32[3,32,512]{2,1,0:T(8,128)} copy(f32[3,32,512]{2,1,0:T(8,128)} %bitcast.4) | data formatting | bytes 393216

commit v5 on v4

--- a/solution.py
+++ b/solution.py
@@ -224,10 +224,7 @@
     scale = 1.0 / (WIN * spread_of)
     for j in range(steps):
         value = (raw[pl.ds(j * count, count), :] - mean) * scale
-        tpl[pl.ds(0, count), pl.ds(j * LANES, LANES)] = value.astype(jnp.bfloat16)
-    tpl[pl.ds(count, LANES - count), :] = jnp.zeros(
-        (LANES - count, tpl.shape[1]), jnp.bfloat16
-    )
+        tpl[:, pl.ds(j * LANES, LANES)] = value.astype(jnp.bfloat16)
 
     core, x, y = lax.rem(place, 2), lax.rem(place // 2, 2), place // 4
     xa, ya = x + (1 - 2 * x) * (1 - core), y + (1 - 2 * y) * core
@@ -251,10 +248,10 @@
 
         for h, block in ((0, block_pair), (1, block_mine)):
             product = lax.dot_general(
-                win[pl.ds(pl.multiple_of(block * samp, samp), samp), :], tpl[...],
+                tpl[...], win[pl.ds(pl.multiple_of(block * samp, samp), samp), :],
                 (((1,), (1,)), ((), ())), preferred_element_type=jnp.float32,
             )
-            part[q, h] = product.T[:count] * factor
+            part[q, h] = product * factor
         copy = remote(part.at[q, 0], pair.at[q], pair_send.at[q], pair_recv.at[q], to_pair)
         copy.start()
         pair_copies.append(copy)
@@ -313,7 +310,7 @@
             pltpu.VMEM((parts, total + TAIL), f32),
             pltpu.VMEM((total + LANES, LANES), f32),
             pltpu.VMEM((24 * count, LANES), f32),
-            pltpu.VMEM((LANES, deep), bf16),
+            pltpu.VMEM((count, deep), bf16),
             pltpu.VMEM((GROUP * samp, LANES), f32),
             pltpu.VMEM((GROUP * samp, deep), bf16),
             pltpu.VMEM((4, 2, count, samp), f32),

time: 47.5 us -> 47.7 us (level)
  no operation moved by 1% of the time
where the time goes in v5:
time: 47.7 us; the launch traced here: 47.5 us
  Pallas kernels  45.9 us (96%)
  local copies, waits for them, and re-layouts  1.62 us (3%)
    pallas_call x1, Pallas kernels, body(): pl.pallas_call(functools.partial(fused_kernel, n, samp, 1.0 / math.sqrt(s...  45.9 us
    unnamed x1, local copies, waits for them, and re-layouts  1.62 us

profile of v5, /device:TPU:0, one launch (start us, length us, event | category | flops | bytes accessed | tf_op | source)
XLA Modules:
  0.0 47.5 jit_solution(9947235375453332670)
XLA Ops:
  0.0 45.9 %shard_map.55 = f32[96,512]{1,0:T(8,128)} custom-call(s32[96]{0:T(128)} %bitcast.7, s32[96]{0:T(128)} %offset_ref.1, f32[192,512]{1,0:T(8,128)} %record_ref.1, s32[1,192]{1,0:T(1,128)} %bitcast.5, s32[1,192]{1,0:T(1,128)} %bitcast.6), custom_call_target="tpu_custom_call" | custom-call | tf_op jit(solution)/shard_map/pallas_call | solution.py:301
  45.9 1.6 %copy.7 = f32[3,32,512]{2,1,0:T(8,128)} copy(f32[3,32,512]{2,1,0:T(8,128)} %bitcast.4) | data formatting | bytes 393216

commit v6 on v5

--- a/solution.py
+++ b/solution.py
@@ -38,7 +38,7 @@
 def fused_kernel(
     n, samp, factor, owner_ref, offset_ref, record_ref, station_ref, valid_ref, out_ref,
     mine, everyone, eye, chan, rows, raw, tpl, gain, win, part, pair, from_a, from_b,
-    send_sem, recv_sem, own_sem, pair_send, pair_recv, a_send, a_recv, b_send, b_recv,
+    send_sem, recv_sem, pass_send, own_sem, pair_send, pair_recv, a_send, a_recv, b_send, b_recv,
 ):
     me = lax.axis_index("tm")
     plane = me // GROUP
@@ -73,17 +73,59 @@
     own.start()
     pl.semaphore_wait(barrier, n - 1)
 
-    def target(d):
-        return lax.rem(base + n - (d // GROUP) * GROUP + lax.rem(place + d, GROUP), n)
-
-    def send(d, carry):
-        to = target(d)
-        remote(
-            mine.at[lax.rem(to, GROUP)], everyone.at[me], send_sem.at[d], recv_sem.at[me], to
-        ).start()
-        return carry
-
-    lax.fori_loop(1, n, send, 0)
+    def arrived(j):
+        remote(mine.at[0], everyone.at[j], send_sem.at[0], recv_sem.at[j], j).wait_recv()
+
+    planes = n // GROUP
+    below, above = plane > 0, plane < planes - 1
+
+    def to_plane(shift, act):
+        def one(d, carry):
+            part_of = lax.rem(place + d, GROUP)
+            act(
+                remote(
+                    mine.at[part_of], everyone.at[me], send_sem.at[(shift + 1) * GROUP + d],
+                    recv_sem.at[me], base + shift * GROUP + part_of,
+                )
+            )
+            return carry
+
+        lax.fori_loop(0 if shift else 1, GROUP, one, 0)
+
+    def all_planes(act):
+        to_plane(0, act)
+        pl.when(below)(lambda: to_plane(-1, act))
+        pl.when(above)(lambda: to_plane(1, act))
+
+    def handed_on(source, to):
+        return remote(
+            everyone.at[source], everyone.at[source], pass_send.at[source],
+            recv_sem.at[source], to,
+        )
+
+    def hand_on(hops, act, wait):
+        def one(d, carry):
+            k = lax.rem(place + d, GROUP)
+
+            @pl.when(plane + hops < planes)
+            def from_above():
+                source = base + hops * GROUP + k
+                if wait:
+                    arrived(source)
+                pl.when(below)(lambda: act(handed_on(source, me - GROUP)))
+
+            @pl.when(plane - hops >= 0)
+            def from_below():
+                source = base - hops * GROUP + k
+                if wait:
+                    arrived(source)
+                pl.when(above)(lambda: act(handed_on(source, me + GROUP)))
+
+            return carry
+
+        lax.fori_loop(0, GROUP, one, 0)
+
+    all_planes(lambda copy: copy.start())
 
     wide = station_ref.shape[1]
     lane = lax.broadcasted_iota(jnp.int32, (parts, wide), 1)
@@ -108,9 +150,6 @@
         chan[:, pl.ds(pl.multiple_of(j * samp, samp), half)] = block[:parts]
         chan[:, pl.ds(pl.multiple_of(j * samp + half, half), half)] = block[parts:]
 
-    def arrived(j):
-        remote(mine.at[0], everyone.at[j], send_sem.at[0], recv_sem.at[j], j).wait_recv()
-
     def turn(at, length):
         values = chan[:, pl.ds(at, length + LANES)]
         pieces = [ahead(values, k)[:, :length] for k in range(SHIFTS)]
@@ -162,32 +201,35 @@
             win[pl.ds(at, sub), pl.ds(j * LANES, LANES)] = (x * scaled).astype(jnp.bfloat16)
         return carry
 
-    early = (GROUP - 2) * samp // sub
+    last = GROUP * samp // sub
+    early = last // 2
+    hand_on(1, lambda copy: copy.start(), True)
     lax.fori_loop(0, GROUP // 2 - 1, gains_two, 0)
     lax.fori_loop(0, early, fill, 0)
+    for hops in range(2, planes - 1):
+        hand_on(hops, lambda copy: copy.start(), True)
     after = lax.rem(base + GROUP, n)
-    arrived(after)
-    spread(after)
+
+    @pl.when(above)
+    def spread_after():
+        spread(after)
+
     turn(pl.multiple_of(first + (GROUP - 1) * samp, samp), samp)
     turn(pl.multiple_of(first + GROUP * samp, samp), LANES)
     gains_two(GROUP // 2 - 1, 0)
-    lax.fori_loop(early, GROUP * samp // sub, fill, 0)
-
-    def take_far(e, blocks):
-        for d in range(blocks):
-            source = lax.rem(base + e + d, n)
-            arrived(source)
-            spread(source)
+    lax.fori_loop(early, last, fill, 0)
+    hand_on(planes - 1, lambda copy: copy.start(), True)
+
+    def take_far(i, carry):
+        e = GROUP + i * 4
+        for d in range(4):
+            spread(lax.rem(base + e + d, n))
         for d in range(4):
             turn(pl.multiple_of(lax.rem(base + e + d - 1, n) * samp, samp), samp)
-
-    def take_four(i, carry):
-        take_far(GROUP + 1 + i * 4, 4)
-        return carry
-
-    far = n - GROUP - 1
-    lax.fori_loop(0, far // 4, take_four, 0)
-    take_far(n - far % 4, far % 4)
+        return carry
+
+    lax.fori_loop(0, (n - GROUP) // 4, take_far, 0)
+    turn(pl.multiple_of(lax.rem(base + n - 1, n) * samp, samp), samp)
     rows[pl.ds(total, LANES), :] = jnp.zeros((LANES, LANES), jnp.float32)
 
     def pick(b, carry):
@@ -277,13 +319,9 @@
     for copy in pair_copies + a_copies + b_copies:
         copy.wait_send()
 
-    def sent(d, carry):
-        remote(
-            mine.at[0], everyone.at[me], send_sem.at[d], recv_sem.at[me], target(d)
-        ).wait_send()
-        return carry
-
-    lax.fori_loop(1, n, sent, 0)
+    all_planes(lambda copy: copy.wait_send())
+    for hops in range(1, planes):
+        hand_on(hops, lambda copy: copy.wait_send(), False)
 
 
 def body(record, owner, offset, station, valid):
@@ -317,7 +355,7 @@
             pltpu.VMEM((4, count, samp), f32),
             pltpu.VMEM((2, count, samp), f32),
             pltpu.VMEM((count, samp), f32),
-            dma((n,)), dma((n,)), dma,
+            dma((3 * GROUP,)), dma((n,)), dma((n,)), dma,
             dma((4,)), dma((4,)), dma((2,)), dma((2,)), dma, dma,
         ],
         compiler_params=pltpu.CompilerParams(

time: 47.7 us -> 49.7 us (1.042)
  Pallas kernels: 45.9 us -> 47.9 us
    pallas_call x1, Pallas kernels: 45.9 us -> 47.9 us  [body(): pl.pallas_call(functools.partial(fused_kernel, n, samp, 1.0 / math.sqrt(s...]
where the time goes in v6:
time: 49.7 us; the launch traced here: 49.6 us
  Pallas kernels  47.9 us (96%)
  local copies, waits for them, and re-layouts  1.62 us (3%)
    pallas_call x1, Pallas kernels, body(): pl.pallas_call(functools.partial(fused_kernel, n, samp, 1.0 / math.sqrt(s...  47.9 us
    unnamed x1, local copies, waits for them, and re-layouts  1.62 us

profile of v6, /device:TPU:0, one launch (start us, length us, event | category | flops | bytes accessed | tf_op | source)
XLA Modules:
  0.0 49.6 jit_solution(14725964525906351311)
XLA Ops:
  0.0 47.9 %shard_map.55 = f32[96,512]{1,0:T(8,128)} custom-call(s32[96]{0:T(128)} %bitcast.7, s32[96]{0:T(128)} %offset_ref.1, f32[192,512]{1,0:T(8,128)} %record_ref.1, s32[1,192]{1,0:T(1,128)} %bitcast.5, s32[1,192]{1,0:T(1,128)} %bitcast.6), custom_call_target="tpu_custom_call" | custom-call | tf_op jit(solution)/shard_map/pallas_call | solution.py:339
  48.0 1.6 %copy.7 = f32[3,32,512]{2,1,0:T(8,128)} copy(f32[3,32,512]{2,1,0:T(8,128)} %bitcast.4) | data formatting | bytes 393216

commit v7 on v5

--- a/solution.py
+++ b/solution.py
@@ -36,8 +36,8 @@
 
 
 def fused_kernel(
-    n, samp, factor, owner_ref, offset_ref, record_ref, station_ref, valid_ref, out_ref,
-    mine, everyone, eye, chan, rows, raw, tpl, gain, win, part, pair, from_a, from_b,
+    n, samp, factor, owner_ref, offset_ref, owner_col_ref, record_ref, station_ref, valid_ref, out_ref,
+    mine, everyone, eye, chan, rows, group, cut, masked, raw, tpl, gain, win, part, pair, from_a, from_b,
     send_sem, recv_sem, own_sem, pair_send, pair_recv, a_send, a_recv, b_send, b_recv,
 ):
     me = lax.axis_index("tm")
@@ -111,18 +111,32 @@
     def arrived(j):
         remote(mine.at[0], everyone.at[j], send_sem.at[0], recv_sem.at[j], j).wait_recv()
 
-    def turn(at, length):
-        values = chan[:, pl.ds(at, length + LANES)]
-        pieces = [ahead(values, k)[:, :length] for k in range(SHIFTS)]
-        pieces.append(jnp.zeros((LANES - rows_in, length), jnp.float32))
-        wide_rows = jnp.concatenate(pieces, axis=0).astype(jnp.bfloat16)
+    def transposed(pieces, dst):
+        length = pieces[0].shape[1]
+        blank = jnp.zeros((LANES - parts * len(pieces), length), jnp.float32)
+        wide_rows = jnp.concatenate(pieces + [blank], axis=0).astype(jnp.bfloat16)
         for cut in range(0, length, 2 * LANES):
             size = min(2 * LANES, length - cut)
-            rows[pl.ds(at + cut, size), :] = lax.dot_general(
+            dst[pl.ds(cut, size), :] = lax.dot_general(
                 eye[pl.ds(0, size), pl.ds(0, size)], wide_rows[:, cut : cut + size],
                 (((1,), (1,)), ((), ())), preferred_element_type=jnp.float32,
             )
 
+    def turn(i, length):
+        values = chan[:, pl.ds(pl.multiple_of(first + i * samp, samp), length + LANES)]
+        transposed(
+            [ahead(values, k)[:, :length] for k in range(SHIFTS)],
+            rows.at[pl.ds(i * samp, length)],
+        )
+
+    def turn_group(g):
+        at = [lax.rem(base + e, n) for e in range(g * SHIFTS, min(n, (g + 1) * SHIFTS))]
+        transposed(
+            [chan[:, pl.ds(pl.multiple_of(b * samp, samp), samp + LANES)] for b in at],
+            group.at[g],
+        )
+
+    first = pl.multiple_of(base * samp, samp)
     own.wait()
     spread(me)
 
@@ -133,10 +147,8 @@
         return carry
 
     lax.fori_loop(1, GROUP, take_plane, 0)
-    first = pl.multiple_of(base * samp, samp)
-
     for i in range(GROUP - 1):
-        turn(pl.multiple_of(first + i * samp, samp), samp)
+        turn(i, samp)
     sub = 64
 
     def gains(at, length):
@@ -158,7 +170,7 @@
         at = pl.multiple_of(r * sub, sub)
         scaled = gain[pl.ds(at, sub), :]
         for j in range(steps):
-            x = rows[pl.ds(first + at + j * SHIFTS, sub), :]
+            x = rows[pl.ds(at + j * SHIFTS, sub), :]
             win[pl.ds(at, sub), pl.ds(j * LANES, LANES)] = (x * scaled).astype(jnp.bfloat16)
         return carry
 
@@ -168,38 +180,51 @@
     after = lax.rem(base + GROUP, n)
     arrived(after)
     spread(after)
-    turn(pl.multiple_of(first + (GROUP - 1) * samp, samp), samp)
-    turn(pl.multiple_of(first + GROUP * samp, samp), LANES)
+    turn(GROUP - 1, samp)
+    turn(GROUP, LANES)
     gains_two(GROUP // 2 - 1, 0)
     lax.fori_loop(early, GROUP * samp // sub, fill, 0)
 
-    def take_far(e, blocks):
-        for d in range(blocks):
-            source = lax.rem(base + e + d, n)
+    taken = GROUP + 1
+    for g in range(pl.cdiv(n, SHIFTS)):
+        needed = min(n, (g + 1) * SHIFTS + 1)
+        for e in range(taken, needed):
+            source = lax.rem(base + e, n)
             arrived(source)
             spread(source)
-        for d in range(4):
-            turn(pl.multiple_of(lax.rem(base + e + d - 1, n) * samp, samp), samp)
-
-    def take_four(i, carry):
-        take_far(GROUP + 1 + i * 4, 4)
-        return carry
-
-    far = n - GROUP - 1
-    lax.fori_loop(0, far // 4, take_four, 0)
-    take_far(n - far % 4, far % 4)
-    rows[pl.ds(total, LANES), :] = jnp.zeros((LANES, LANES), jnp.float32)
+        taken = max(taken, needed)
+        turn_group(g)
 
     def pick(b, carry):
-        found = []
-        for t in range(8):
-            start = owner_ref[b * 8 + t] * samp + offset_ref[b * 8 + t]
-            found.append(rows[pl.ds(start, 24, stride=SHIFTS), :])
-        for t in range(8):
-            raw[pl.ds(b * 8 + t, 24, stride=count), :] = found[t]
-        return carry
-
-    lax.fori_loop(0, count // 8, pick, 0)
+        for t in range(4):
+            row = b * 4 + t
+            after_base = lax.rem(owner_ref[row] + (n - base), n)
+            g, begin = lax.div(after_base, jnp.int32(SHIFTS)), offset_ref[row]
+            found = [group[g, pl.ds(begin + k, 24, stride=SHIFTS), :] for k in range(SHIFTS)]
+            for k in range(SHIFTS):
+                cut[k, pl.ds(row, 24, stride=count), :] = found[k]
+        return carry
+
+    lax.fori_loop(0, count // 4, pick, 0)
+    held = lax.rem(lax.rem(owner_col_ref[...] + (n - base), n), jnp.int32(SHIFTS))
+    lanes_of = lax.broadcasted_iota(jnp.int32, (count, LANES), 1)
+    low = held * parts
+    wanted = (lanes_of >= low) & (lanes_of < low + parts)
+    for j in range(steps):
+        for k in range(SHIFTS):
+            value = jnp.where(wanted, cut[k, pl.ds(j * count, count), :], 0.0)
+            masked[pl.ds(j * count, count), pl.ds(k * LANES, LANES)] = value.astype(jnp.bfloat16)
+    from_lane = lax.broadcasted_iota(jnp.int32, (SHIFTS * LANES, LANES), 0)
+    to_lane = lax.broadcasted_iota(jnp.int32, (SHIFTS * LANES, LANES), 1)
+    moves = (
+        (lax.rem(lax.rem(from_lane, LANES), parts) == lax.rem(to_lane, parts))
+        & (lax.div(from_lane, LANES) == lax.div(to_lane, parts))
+        & (lax.rem(from_lane, LANES) < rows_in)
+    )
+    raw[...] = jnp.dot(
+        masked[...], jnp.where(moves, 1.0, 0.0).astype(jnp.bfloat16),
+        preferred_element_type=jnp.float32,
+    )
     lane_a = lax.broadcasted_iota(jnp.int32, (LANES, LANES), 0)
     lane_b = lax.broadcasted_iota(jnp.int32, (LANES, LANES), 1)
     same = (lax.rem(lane_a, parts) == lax.rem(lane_b, parts)) & (
@@ -301,15 +326,18 @@
     stack = pl.pallas_call(
         functools.partial(fused_kernel, n, samp, 1.0 / math.sqrt(stations)),
         out_shape=jax.ShapeDtypeStruct((count, samp), f32),
-        in_specs=[SMEM, SMEM, VMEM, VMEM, VMEM],
+        in_specs=[SMEM, SMEM, VMEM, VMEM, VMEM, VMEM],
         out_specs=VMEM,
         scratch_shapes=[
             pltpu.VMEM((GROUP, 2 * parts, samp // 2), bf16),
             pltpu.VMEM((n, 2 * parts, samp // 2), bf16),
             pltpu.VMEM((2 * LANES, 2 * LANES), bf16),
             pltpu.VMEM((parts, total + TAIL), f32),
-            pltpu.VMEM((total + LANES, LANES), f32),
-            pltpu.VMEM((24 * count, LANES), f32),
+            pltpu.VMEM((GROUP * samp + LANES, LANES), f32),
+            pltpu.VMEM((pl.cdiv(n, SHIFTS), samp + LANES, LANES), f32),
+            pltpu.VMEM((SHIFTS, 24 * count, LANES), f32),
+            pltpu.VMEM((WIN // SHIFTS * count, SHIFTS * LANES), bf16),
+            pltpu.VMEM((WIN // SHIFTS * count, LANES), f32),
             pltpu.VMEM((count, deep), bf16),
             pltpu.VMEM((GROUP * samp, LANES), f32),
             pltpu.VMEM((GROUP * samp, deep), bf16),
@@ -323,7 +351,7 @@
         compiler_params=pltpu.CompilerParams(
             collective_id=0, has_side_effects=True, vmem_limit_bytes=56 * 1024 * 1024
         ),
-    )(owner.reshape(-1), offset, record, station[None, :], valid[None, :])
+    )(owner.reshape(-1), offset, owner, record, station[None, :], valid[None, :])
     stack = stack.reshape(NSTEP, TPL_STEP, samp)
     return lax.psum_scatter(stack, "sta", scatter_dimension=1, tiled=True)
 

time: 47.7 us -> 53.5 us (1.12)
  Pallas kernels: 45.9 us -> 50.4 us
  local copies, waits for them, and re-layouts: 1.62 us -> 2.99 us
    pallas_call x1, Pallas kernels: 45.9 us -> 50.4 us  [body(): pl.pallas_call(functools.partial(fused_kernel, n, samp, 1.0 / math.sqrt(s...]
    unnamed x1 -> x4, local copies, waits for them, and re-layouts: 1.62 us -> 2.99 us
where the time goes in v7:
time: 53.5 us; the launch traced here: 53.4 us
  Pallas kernels  50.4 us (94%)
  local copies, waits for them, and re-layouts  2.99 us (6%)
    pallas_call x1, Pallas kernels, body(): pl.pallas_call(functools.partial(fused_kernel, n, samp, 1.0 / math.sqrt(s...  50.4 us
    unnamed x4, local copies, waits for them, and re-layouts  2.99 us

profile of v7, /device:TPU:0, one launch (start us, length us, event | category | flops | bytes accessed | tf_op | source)
XLA Modules:
  0.0 53.4 jit_solution(10030285968564396806)
XLA Ops:
  0.0 0.0 copy-start
  0.0 0.7 %copy-done = s32[96,1]{0,1:T(1,128)S(1)} copy-done((s32[96,1]{0,1:T(1,128)S(1)}, s32[96,1]{0,1:T(1,128)}, u32[]{:S(2)}) %copy-start) | copy-done | bytes 408
  0.7 0.7 %copy.6.owner_col_ref = s32[96,1]{1,0:T(8,128)} copy(s32[96,1]{0,1:T(1,128)S(1)} %copy-done) | data formatting | bytes 768 | tf_op args[1]
  1.4 50.4 %shard_map.55 = f32[96,512]{1,0:T(8,128)} custom-call(s32[96]{0:T(128)} %bitcast.5, s32[96]{0:T(128)} %offset_ref.1, s32[96,1]{1,0:T(8,128)} %copy.6.owner_col_ref, f32[192,512]{1,0:T(8,128)} %record_ref.1, s32[1,192]{1,0:T(1,128)} %bitcast.6, s32[1,192]{1,0:T(1,128)} %bitcast.7), custom_call_target="tpu_custom_call" | custom-call | tf_op jit(solution)/shard_map/pallas_call | solution.py:326
  51.7 1.6 %copy.8 = f32[3,32,512]{2,1,0:T(8,128)} copy(f32[3,32,512]{2,1,0:T(8,128)} %bitcast.4) | data formatting | bytes 393216
Async XLA Ops:
  0.0 0.7 %copy-start = (s32[96,1]{0,1:T(1,128)S(1)}, s32[96,1]{0,1:T(1,128)}, u32[]{:S(2)}) copy-start(s32[96,1]{0,1:T(1,128)} %param.6) | copy-start | bytes 1156

commit v8 on v6

--- a/solution.py
+++ b/solution.py
@@ -16,6 +16,7 @@
 SHIFTS = 5
 LANES = 128
 TAIL = 256
+ODD = 25
 MESH = pl.DeviceIdType.MESH
 VMEM = pl.BlockSpec(memory_space=pltpu.VMEM)
 SMEM = pl.BlockSpec(memory_space=pltpu.SMEM)
@@ -203,45 +204,74 @@
 
     last = GROUP * samp // sub
     early = last // 2
-    hand_on(1, lambda copy: copy.start(), True)
+
+    def start(copy):
+        copy.start()
+
+    def turn_block(block):
+        turn(pl.multiple_of(block * samp, samp), samp)
+
+    def take_four(block, lag, wait):
+        for d in range(4):
+            if wait:
+                arrived(block + d)
+            spread(block + d)
+        for d in range(4):
+            turn_block(block + d - lag)
+
+    def take_planes(hops, wait):
+        @pl.when(plane + hops < planes)
+        def from_above():
+            head = base + hops * GROUP
+
+            def four(i, carry):
+                take_four(head + i * 4, 1, wait)
+                return carry
+
+            lax.fori_loop(0, GROUP // 4, four, 0)
+            pl.when(plane + hops == planes - 1)(lambda: turn_block(head + GROUP - 1))
+
+        @pl.when(plane - hops >= 0)
+        def from_below():
+            head = base - hops * GROUP
+
+            def four(i, carry):
+                at = head + (GROUP // 4 - 1 - i) * 4
+                take_four(at, 0, wait)
+                return carry
+
+            lax.fori_loop(0, GROUP // 4, four, 0)
+
+    hand_on(1, start, True)
     lax.fori_loop(0, GROUP // 2 - 1, gains_two, 0)
     lax.fori_loop(0, early, fill, 0)
     for hops in range(2, planes - 1):
-        hand_on(hops, lambda copy: copy.start(), True)
-    after = lax.rem(base + GROUP, n)
-
-    @pl.when(above)
-    def spread_after():
-        spread(after)
-
+        hand_on(hops, start, True)
+    pl.when(above)(lambda: spread(lax.rem(base + GROUP, n)))
     turn(pl.multiple_of(first + (GROUP - 1) * samp, samp), samp)
     turn(pl.multiple_of(first + GROUP * samp, samp), LANES)
     gains_two(GROUP // 2 - 1, 0)
+    take_planes(1, False)
     lax.fori_loop(early, last, fill, 0)
-    hand_on(planes - 1, lambda copy: copy.start(), True)
-
-    def take_far(i, carry):
-        e = GROUP + i * 4
-        for d in range(4):
-            spread(lax.rem(base + e + d, n))
-        for d in range(4):
-            turn(pl.multiple_of(lax.rem(base + e + d - 1, n) * samp, samp), samp)
-        return carry
-
-    lax.fori_loop(0, (n - GROUP) // 4, take_far, 0)
-    turn(pl.multiple_of(lax.rem(base + n - 1, n) * samp, samp), samp)
+    for hops in range(2, planes - 1):
+        take_planes(hops, False)
+    take_planes(planes - 1, True)
     rows[pl.ds(total, LANES), :] = jnp.zeros((LANES, LANES), jnp.float32)
 
     def pick(b, carry):
         found = []
         for t in range(8):
-            start = owner_ref[b * 8 + t] * samp + offset_ref[b * 8 + t]
-            found.append(rows[pl.ds(start, 24, stride=SHIFTS), :])
+            begin = owner_ref[b * 8 + t] * samp + offset_ref[b * 8 + t]
+            found.append(rows[pl.ds(begin, 24, stride=SHIFTS), :])
         for t in range(8):
-            raw[pl.ds(b * 8 + t, 24, stride=count), :] = found[t]
+            raw[pl.ds((b * 8 + t) * ODD, 24), :] = found[t]
         return carry
 
     lax.fori_loop(0, count // 8, pick, 0)
+
+    def row_of(j):
+        return raw[pl.ds(j, count, stride=ODD), :]
+
     lane_a = lax.broadcasted_iota(jnp.int32, (LANES, LANES), 0)
     lane_b = lax.broadcasted_iota(jnp.int32, (LANES, LANES), 1)
     same = (lax.rem(lane_a, parts) == lax.rem(lane_b, parts)) & (
@@ -254,18 +284,18 @@
             x, fold, precision=lax.Precision.HIGHEST, preferred_element_type=jnp.float32
         )
 
-    sums = raw[pl.ds(0, count), :]
+    sums = row_of(0)
     for j in range(1, steps):
-        sums = sums + raw[pl.ds(j * count, count), :]
+        sums = sums + row_of(j)
     mean = folded(sums) / WIN
     square = jnp.zeros_like(mean)
     for j in range(steps):
-        centred = raw[pl.ds(j * count, count), :] - mean
+        centred = row_of(j) - mean
         square = square + centred * centred
     spread_of = jnp.sqrt(folded(square) / WIN + EPSILON)
     scale = 1.0 / (WIN * spread_of)
     for j in range(steps):
-        value = (raw[pl.ds(j * count, count), :] - mean) * scale
+        value = (row_of(j) - mean) * scale
         tpl[:, pl.ds(j * LANES, LANES)] = value.astype(jnp.bfloat16)
 
     core, x, y = lax.rem(place, 2), lax.rem(place // 2, 2), place // 4
@@ -347,7 +377,7 @@
             pltpu.VMEM((2 * LANES, 2 * LANES), bf16),
             pltpu.VMEM((parts, total + TAIL), f32),
             pltpu.VMEM((total + LANES, LANES), f32),
-            pltpu.VMEM((24 * count, LANES), f32),
+            pltpu.VMEM((ODD * count, LANES), f32),
             pltpu.VMEM((count, deep), bf16),
             pltpu.VMEM((GROUP * samp, LANES), f32),
             pltpu.VMEM((GROUP * samp, deep), bf16),

time: 49.7 us -> 47 us (0.946)
  Pallas kernels: 47.9 us -> 45.2 us
    pallas_call x1, Pallas kernels: 47.9 us -> 45.2 us  [body(): pl.pallas_call(functools.partial(fused_kernel, n, samp, 1.0 / math.sqrt(s...]
where the time goes in v8:
time: 47 us; the launch traced here: 46.8 us
  Pallas kernels  45.2 us (96%)
  local copies, waits for them, and re-layouts  1.62 us (3%)
    pallas_call x1, Pallas kernels, body(): pl.pallas_call(functools.partial(fused_kernel, n, samp, 1.0 / math.sqrt(s...  45.2 us
    unnamed x1, local copies, waits for them, and re-layouts  1.62 us

profile of v8, /device:TPU:0, one launch (start us, length us, event | category | flops | bytes accessed | tf_op | source)
XLA Modules:
  0.0 46.8 jit_solution(15776050857077665446)
XLA Ops:
  0.0 45.2 %shard_map.55 = f32[96,512]{1,0:T(8,128)} custom-call(s32[96]{0:T(128)} %bitcast.7, s32[96]{0:T(128)} %offset_ref.1, f32[192,512]{1,0:T(8,128)} %record_ref.1, s32[1,192]{1,0:T(1,128)} %bitcast.5, s32[1,192]{1,0:T(1,128)} %bitcast.6), custom_call_target="tpu_custom_call" | custom-call | tf_op jit(solution)/shard_map/pallas_call | solution.py:369
  45.2 1.6 %copy.7 = f32[3,32,512]{2,1,0:T(8,128)} copy(f32[3,32,512]{2,1,0:T(8,128)} %bitcast.4) | data formatting | bytes 393216

commit v9 on v8

--- a/solution.py
+++ b/solution.py
@@ -194,16 +194,29 @@
         gains(pl.multiple_of(first + i * (2 * samp), samp), 2 * samp)
         return carry
 
-    def fill(r, carry):
-        at = pl.multiple_of(r * sub, sub)
-        scaled = gain[pl.ds(at, sub), :]
-        for j in range(steps):
-            x = rows[pl.ds(first + at + j * SHIFTS, sub), :]
-            win[pl.ds(at, sub), pl.ds(j * LANES, LANES)] = (x * scaled).astype(jnp.bfloat16)
-        return carry
-
-    last = GROUP * samp // sub
-    early = last // 2
+    core, x, y = lax.rem(place, 2), lax.rem(place // 2, 2), place // 4
+    xa, ya = x + (1 - 2 * x) * (1 - core), y + (1 - 2 * y) * core
+    xb, yb = x + (1 - 2 * x) * core, y + (1 - 2 * y) * (1 - core)
+    own_chip, chip_a, chip_b = y * 2 + x, ya * 2 + xa, yb * 2 + xb
+    diagonal = (1 - y) * 2 + (1 - x)
+    mine_order = [diagonal, chip_a, chip_b, own_chip]
+    pair_order = [diagonal, chip_b, chip_a, own_chip]
+
+    def fill(q, r):
+        for h, block in ((0, pair_order[q] * 2 + (1 - core)), (1, mine_order[q] * 2 + core)):
+            at = pl.multiple_of(block * samp + r * sub, sub)
+            to = r * sub if isinstance(r, int) else pl.multiple_of(r * sub, sub)
+            scaled = gain[pl.ds(at, sub), :]
+            for j in range(steps):
+                value = rows[pl.ds(first + at + j * SHIFTS, sub), :] * scaled
+                win[q * 2 + h, pl.ds(to, sub), pl.ds(j * LANES, LANES)] = value.astype(jnp.bfloat16)
+
+    def fill_pair(q):
+        def one(r, carry):
+            fill(q, r)
+            return carry
+
+        lax.fori_loop(0, samp // sub, one, 0)
 
     def start(copy):
         copy.start()
@@ -243,16 +256,15 @@
             lax.fori_loop(0, GROUP // 4, four, 0)
 
     hand_on(1, start, True)
-    lax.fori_loop(0, GROUP // 2 - 1, gains_two, 0)
-    lax.fori_loop(0, early, fill, 0)
-    for hops in range(2, planes - 1):
-        hand_on(hops, start, True)
     pl.when(above)(lambda: spread(lax.rem(base + GROUP, n)))
     turn(pl.multiple_of(first + (GROUP - 1) * samp, samp), samp)
     turn(pl.multiple_of(first + GROUP * samp, samp), LANES)
-    gains_two(GROUP // 2 - 1, 0)
+    lax.fori_loop(0, GROUP // 2, gains_two, 0)
+    fill_pair(0)
+    for hops in range(2, planes - 1):
+        hand_on(hops, start, True)
     take_planes(1, False)
-    lax.fori_loop(early, last, fill, 0)
+    fill_pair(1)
     for hops in range(2, planes - 1):
         take_planes(hops, False)
     take_planes(planes - 1, True)
@@ -298,13 +310,6 @@
         value = (row_of(j) - mean) * scale
         tpl[:, pl.ds(j * LANES, LANES)] = value.astype(jnp.bfloat16)
 
-    core, x, y = lax.rem(place, 2), lax.rem(place // 2, 2), place // 4
-    xa, ya = x + (1 - 2 * x) * (1 - core), y + (1 - 2 * y) * core
-    xb, yb = x + (1 - 2 * x) * core, y + (1 - 2 * y) * (1 - core)
-    own_chip, chip_a, chip_b = y * 2 + x, ya * 2 + xa, yb * 2 + xb
-    diagonal = (1 - y) * 2 + (1 - x)
-    mine_order = [diagonal, chip_a, chip_b, own_chip]
-    pair_order = [diagonal, chip_b, chip_a, own_chip]
     to_pair = base + own_chip * 2 + (1 - core)
     to_a = base + chip_a * 2 + core
     to_b = base + chip_b * 2 + core
@@ -315,15 +320,15 @@
         part[q, 1] += pair[q]
 
     for q in range(4):
-        block_pair = pair_order[q] * 2 + (1 - core)
-        block_mine = mine_order[q] * 2 + core
-
-        for h, block in ((0, block_pair), (1, block_mine)):
+        for h in range(2):
             product = lax.dot_general(
-                tpl[...], win[pl.ds(pl.multiple_of(block * samp, samp), samp), :],
-                (((1,), (1,)), ((), ())), preferred_element_type=jnp.float32,
+                tpl[...], win[q * 2 + h], (((1,), (1,)), ((), ())),
+                preferred_element_type=jnp.float32,
             )
             part[q, h] = product * factor
+        if q < 2:
+            for r in range(samp // sub):
+                fill(q + 2, r)
         copy = remote(part.at[q, 0], pair.at[q], pair_send.at[q], pair_recv.at[q], to_pair)
         copy.start()
         pair_copies.append(copy)
@@ -380,7 +385,7 @@
             pltpu.VMEM((ODD * count, LANES), f32),
             pltpu.VMEM((count, deep), bf16),
             pltpu.VMEM((GROUP * samp, LANES), f32),
-            pltpu.VMEM((GROUP * samp, deep), bf16),
+            pltpu.VMEM((GROUP, samp, deep), bf16),
             pltpu.VMEM((4, 2, count, samp), f32),
             pltpu.VMEM((4, count, samp), f32),
             pltpu.VMEM((2, count, samp), f32),

time: 47 us -> 47.7 us (1.015)
  Pallas kernels: 45.2 us -> 45.9 us
    pallas_call x1, Pallas kernels: 45.2 us -> 45.9 us  [body(): pl.pallas_call(functools.partial(fused_kernel, n, samp, 1.0 / math.sqrt(s...]
where the time goes in v9:
time: 47.7 us; the launch traced here: 47.5 us
  Pallas kernels  45.9 us (96%)
  local copies, waits for them, and re-layouts  1.62 us (3%)
    pallas_call x1, Pallas kernels, body(): pl.pallas_call(functools.partial(fused_kernel, n, samp, 1.0 / math.sqrt(s...  45.9 us
    unnamed x1, local copies, waits for them, and re-layouts  1.62 us

profile of v9, /device:TPU:0, one launch (start us, length us, event | category | flops | bytes accessed | tf_op | source)
XLA Modules:
  0.0 47.5 jit_solution(3534775353847080950)
XLA Ops:
  0.0 45.9 %shard_map.55 = f32[96,512]{1,0:T(8,128)} custom-call(s32[96]{0:T(128)} %bitcast.7, s32[96]{0:T(128)} %offset_ref.1, f32[192,512]{1,0:T(8,128)} %record_ref.1, s32[1,192]{1,0:T(1,128)} %bitcast.5, s32[1,192]{1,0:T(1,128)} %bitcast.6), custom_call_target="tpu_custom_call" | custom-call | tf_op jit(solution)/shard_map/pallas_call | solution.py:374
  45.9 1.6 %copy.7 = f32[3,32,512]{2,1,0:T(8,128)} copy(f32[3,32,512]{2,1,0:T(8,128)} %bitcast.4) | data formatting | bytes 393216
